TPU v7x, 128 devices: a whole 4x4x4 slice. The times are simulated.
128 devices in a mesh: lon: 16 (over x_lo, y, core), lat: 8 (over z, x_hi).
Axes of the slice: x: 4 (x_hi: 2, x_lo: 2; x = x_hi * 2 + x_lo), y: 4, z: 4, core: 2. Of those that a mesh axis runs over, the one named last changes fastest.
Arguments:
- input_field: bfloat16 [64, 512, 2048], P(None, 'lat', 'lon'), may hold values from -6 to 6
- conv_first: bfloat16 [3, 3, 128, 64], replicated, may hold values from -0.4375 to 0.4375
- conv_rest: bfloat16 [3, 3, 3, 128, 128], replicated, may hold values from -0.3125 to 0.3125
- flag_patch: int32 [8, 16, 32], P('lat', 'lon'), may hold values from 0 to 31, as said below
- flag_count: int32 [8, 16], P('lat', 'lon'), may hold values from 0 to 32, as said below
- w_embed: bfloat16 [2048, 1024], replicated, may hold values from -0.125 to 0.125
- pos_embed: bfloat16 [16, 1024], replicated, may hold values from -3 to 3
- token_mix: bfloat16 [16, 16], replicated, may hold values from -1.5 to 1.5
- w_up: bfloat16 [1024, 4096], replicated, may hold values from -0.1875 to 0.1875
- w_down: bfloat16 [4096, 1024], replicated, may hold values from -0.09375 to 0.09375
- w_head: bfloat16 [1024, 8], replicated, may hold values from -0.1875 to 0.1875
Outputs:
- features: bfloat16 [512, 2048, 128], P('lat', 'lon')
- flag_scores: float32 [8, 16, 32, 8], P('lat', 'lon')
Inputs may be any that keep to these rules, and one draw needn't show every extreme that they name: `flag_patch`: within a tile the 32 entries are distinct; only the first flag_count entries of a tile are live. `flag_count`: in each latitude band the counts of the tiles sum to 256 minus 1 to 15; some tile of every band has 32.
All inputs are finite; a program needn't handle non-finite values.
Results may differ from a plain program's by a relative error of at most 0.011.
Values may be sent and summed in bfloat16 or wider, within the bound.
A program may use at most 128 MiB of HBM per device.

v0:
```python
import functools

import jax
import jax.numpy as jnp
from jax import lax
from jax.experimental import pallas as pl
from jax.experimental.pallas import tpu as pltpu
from jax.sharding import PartitionSpec as P

BF = jnp.bfloat16
F32 = jnp.float32
MESH = pl.DeviceIdType.MESH

W = 9
Q = W + 2
S = 16
COLS = W * S
PITCH = 152
NEG = (((1,), (1,)), ((), ()))


def halo_kernel(x_ref, p_ref, xf, fx, row_up, row_dn, colf, col_l, col_r,
                r_bot, r_top, r_right, r_left, r_br, r_bl, r_tr, r_tl, send_sem, recv_sem):
    lon = lax.axis_index("lon")
    lat = lax.axis_index("lat")
    n_lon = lax.axis_size("lon")
    n_lat = lax.axis_size("lat")
    west = lax.rem(lon + n_lon - 1, n_lon)
    east = lax.rem(lon + 1, n_lon)
    north = lax.rem(lat + n_lat - 1, n_lat)
    south = lax.rem(lat + 1, n_lat)
    barrier = pltpu.get_barrier_semaphore()
    places = ((lon, north), (lon, south), (west, lat), (east, lat),
              (west, north), (east, north), (west, south), (east, south))
    for place in places:
        pl.semaphore_signal(barrier, inc=1, device_id=place, device_id_type=MESH)

    xf[...] = x_ref[...].astype(F32).reshape(64 * 64, 128)
    ii = lax.broadcasted_iota(jnp.int32, (128, 128), 0)
    jj = lax.broadcasted_iota(jnp.int32, (128, 128), 1)
    eye = (ii == jj).astype(BF)

    def turn(k):
        rows = jnp.concatenate(
            [xf[pl.ds(2 * k, 64, 64), :], xf[pl.ds(2 * k + 1, 64, 64), :]], axis=0
        ).astype(BF)
        cells = lax.dot_general(eye, rows, NEG, preferred_element_type=F32)
        fx[k + 2, 4:132, :] = cells
        colf[0, pl.ds(pl.multiple_of(4 * k, 4), 4), :] = cells[0:4]
        colf[1, pl.ds(pl.multiple_of(4 * k, 4), 4), :] = cells[124:128]

    @pl.loop(0, 32)
    def _(k):
        turn(k)

    row_up[...] = fx[2:4, 4:132, :].astype(BF)
    row_dn[...] = fx[32:34, 4:132, :].astype(BF)
    col_l[...] = colf[0].astype(BF)
    col_r[...] = colf[1].astype(BF)
    pl.semaphore_wait(barrier, 8)
    sends = (
        (row_up, r_bot), (row_dn, r_top), (col_l, r_right), (col_r, r_left),
        (col_l.at[0:16], r_br), (col_r.at[0:16], r_bl),
        (col_l.at[112:128], r_tr), (col_r.at[112:128], r_tl),
    )
    copies = []
    for i, ((src, dst), place) in enumerate(zip(sends, places)):
        copies.append(pltpu.make_async_remote_copy(
            src_ref=src, dst_ref=dst, send_sem=send_sem.at[i], recv_sem=recv_sem.at[i],
            device_id=place, device_id_type=MESH,
        ))
        copies[-1].start()
    for copy in copies:
        copy.wait()

    fx[0:2, 4:132, :] = r_top[...].astype(F32)
    fx[34:36, 4:132, :] = r_bot[...].astype(F32)
    colf[0] = r_left[...].astype(F32)
    colf[1] = r_right[...].astype(F32)

    @pl.loop(0, 32)
    def _(k):
        fx[k + 2, 0:4, :] = colf[0, pl.ds(pl.multiple_of(4 * k, 4), 4), :]
        fx[k + 2, 132:136, :] = colf[1, pl.ds(pl.multiple_of(4 * k, 4), 4), :]

    tl = r_tl[...].astype(F32)
    tr = r_tr[...].astype(F32)
    bl = r_bl[...].astype(F32)
    br = r_br[...].astype(F32)
    for h in range(2):
        fx[h, 0:4, :] = tl[8 + 4 * h:12 + 4 * h]
        fx[h, 132:136, :] = tr[8 + 4 * h:12 + 4 * h]
        fx[34 + h, 0:4, :] = bl[4 * h:4 * h + 4]
        fx[34 + h, 132:136, :] = br[4 * h:4 * h + 4]

    @pl.when(lat == 0)
    def _():
        fx[0:2, :, :] = jnp.zeros((2, PITCH, 128), F32)

    @pl.when(lat == n_lat - 1)
    def _():
        fx[34:36, :, :] = jnp.zeros((2, PITCH, 128), F32)

    @pl.loop(0, 36)
    def _(k):
        for q in range(Q):
            p_ref[k, q] = fx[k, pl.ds(q, S, W), :].astype(BF)


def exchange(x):
    scratch = [
        pltpu.VMEM((64 * 64, 128), F32),
        pltpu.VMEM((36, PITCH, 128), F32),
        pltpu.VMEM((2, 128, 128), BF),
        pltpu.VMEM((2, 128, 128), BF),
        pltpu.VMEM((2, 128, 128), F32),
        pltpu.VMEM((128, 128), BF),
        pltpu.VMEM((128, 128), BF),
        pltpu.VMEM((2, 128, 128), BF),
        pltpu.VMEM((2, 128, 128), BF),
        pltpu.VMEM((128, 128), BF),
        pltpu.VMEM((128, 128), BF),
        pltpu.VMEM((16, 128), BF),
        pltpu.VMEM((16, 128), BF),
        pltpu.VMEM((16, 128), BF),
        pltpu.VMEM((16, 128), BF),
        pltpu.SemaphoreType.DMA((8,)),
        pltpu.SemaphoreType.DMA((8,)),
    ]
    return pl.pallas_call(
        halo_kernel,
        out_shape=jax.ShapeDtypeStruct((36, Q, S, 128), BF),
        in_specs=[pl.BlockSpec(memory_space=pltpu.VMEM)],
        out_specs=pl.BlockSpec(memory_space=pltpu.VMEM),
        scratch_shapes=scratch,
        compiler_params=pltpu.CompilerParams(
            collective_id=0, has_side_effects=True, vmem_limit_bytes=24 * 2**20
        ),
        name="halo",
    )(x)


def silu(v):
    half = 0.5 * v
    return half + half * jnp.tanh(half)


def gelu(v):
    inner = 0.7978845608028654 * (v + 0.044715 * (v * v * v))
    half = 0.5 * v
    return half + half * jnp.tanh(inner)


def norm(v):
    centred = v - jnp.mean(v, axis=-1, keepdims=True)
    return centred * lax.rsqrt(jnp.mean(centred * centred, axis=-1, keepdims=True) + 1e-05)


def main_kernel(p_ref, first_ref, rest_ref, patch_ref, count_ref, pos_ref, mix_ref, head_ref,
                embed_hbm, up_hbm, down_hbm, feat_hbm, score_ref,
                wt1, wts, xa, xb, f4, fo, tok, embed_v, up_v, down_v, tokens_v, normed_v,
                hidden_v, pooled_v, sc_v, wsem, fsem):
    lat = lax.axis_index("lat")
    n_lat = lax.axis_size("lat")
    loads = [
        pltpu.make_async_copy(embed_hbm, embed_v, wsem.at[0]),
        pltpu.make_async_copy(up_hbm, up_v, wsem.at[1]),
        pltpu.make_async_copy(down_hbm, down_v, wsem.at[2]),
    ]
    for load in loads:
        load.start()

    for ro in range(2):
        for p in range(2):
            for dq in range(3):
                blocks = []
                for half in range(2):
                    a = 2 * p + half - ro
                    blocks.append(first_ref[a * 3 + dq] if 0 <= a < 3 else jnp.zeros((128, 64), BF))
                    at = ((p * 3 + dq) * 2 + half) * 128
                    for l in range(3):
                        wts[l, ro * 128:ro * 128 + 128, at:at + 128] = (
                            rest_ref[l * 9 + a * 3 + dq] if 0 <= a < 3 else jnp.zeros((128, 128), BF)
                        )
                at = (p * 3 + dq) * 128
                wt1[ro * 128:ro * 128 + 128, at:at + 128] = jnp.concatenate(blocks, axis=1)

    def window(src, k, r):
        slabs = []
        for p in range(2):
            for dq in range(3):
                part = src[pl.ds(k + p, r), dq:dq + W]
                slabs.append(part.reshape(r * COLS, part.shape[-1]))
        return jnp.concatenate(slabs, axis=1)

    def conv(src, k, r, weights):
        summed = lax.dot_general(window(src, k, r), weights, NEG, preferred_element_type=F32)
        return silu(summed).reshape(r, W, S, 256)

    def layer(src, dst, weights, pairs, r):
        def chunk(k, n):
            y = conv(src, k, n, weights[...])
            dst[pl.ds(k, n), 0:W] = y.astype(BF)
            for e in range(2):
                for i in range(n):
                    dst[k + i, W + e] = pltpu.roll(y[i, e], S - 1, 0).astype(BF)

        @pl.loop(0, pairs // r)
        def _(step):
            chunk(step * r, r)

        if pairs % r:
            chunk(pairs - pairs % r, pairs % r)

    def blank(dst, pair, lo, hi):
        dst[pair, :, :, lo:hi] = jnp.zeros((Q, S, hi - lo), BF)

    layer(p_ref, xa, wt1, 35, 5)

    @pl.when(lat == 0)
    def _():
        blank(xa, 0, 0, 256)
        blank(xa, 1, 0, 128)

    @pl.when(lat == n_lat - 1)
    def _():
        blank(xa, 33, 128, 256)
        blank(xa, 34, 0, 256)

    layer(xa, xb, wts.at[0], 34, 4)

    @pl.when(lat == 0)
    def _():
        blank(xb, 0, 0, 256)

    @pl.when(lat == n_lat - 1)
    def _():
        blank(xb, 33, 0, 256)

    layer(xb, xa, wts.at[1], 33, 4)

    @pl.when(lat == 0)
    def _():
        blank(xa, 0, 0, 128)

    @pl.when(lat == n_lat - 1)
    def _():
        blank(xa, 32, 128, 256)

    def feat_copy(step):
        return pltpu.make_async_copy(
            fo.at[pl.ds(step * 8, 8)], feat_hbm.at[pl.ds(step * 8, 8)], fsem
        )

    @pl.loop(0, 8)
    def _(step):
        y = conv(xa, step * 4, 4, wts[2])
        for i in range(4):
            for half in range(2):
                for q in range(W):
                    f4[i * 2 + half, pl.ds(q, S, W), :] = y[i, q, :, half * 128:half * 128 + 128]
        for row in range(8):
            fo[step * 8 + row] = f4[row, 0:128, :].astype(BF)
        feat_copy(step).start()
        for ar in range(2):
            for b2 in range(2):
                at = pl.multiple_of(step * 64 + ar * 32 + b2 * 16, 16)
                for u in range(4):
                    for v in range(4):
                        two = [f4[ar * 4 + u, pl.ds(4 * (2 * b2 + b) + v, 8, 16), :] for b in range(2)]
                        lane = (u * 4 + v) * 128
                        tok[pl.ds(at, 16), lane:lane + 128] = jnp.concatenate(two, axis=0).astype(BF)

    loads[0].wait()

    @pl.loop(0, 4)
    def _(n):
        lanes = pl.ds(pl.multiple_of(n * 256, 256), 256)
        summed = jnp.dot(tok[...], embed_v[:, lanes], preferred_element_type=F32)
        place = pos_ref[:, lanes].astype(F32)
        wide = summed.reshape(4, 16, 8, 256) + place[None, :, None, :]
        tokens_v[:, lanes] = wide.reshape(512, 256).astype(BF)

    ti = lax.broadcasted_iota(jnp.int32, (128, 16), 0) // 8
    tj = lax.broadcasted_iota(jnp.int32, (128, 16), 1)
    pick = (ti == tj).astype(BF)
    spread = jnp.dot(pick, mix_ref[...], preferred_element_type=F32).astype(BF)
    spread = lax.dot_general(spread, pick, NEG, preferred_element_type=F32)
    ri = lax.broadcasted_iota(jnp.int32, (128, 128), 0) % 8
    rj = lax.broadcasted_iota(jnp.int32, (128, 128), 1) % 8
    mix = jnp.where(ri == rj, spread, 0.0).astype(BF)

    @pl.loop(0, 4)
    def _(pi):
        rows = pl.ds(pl.multiple_of(pi * 128, 128), 128)
        wide = tokens_v[rows, :].astype(F32)
        mixing = jnp.dot(mix, norm(wide).astype(BF), preferred_element_type=F32)
        mixed = (wide + mixing).astype(BF)
        tokens_v[rows, :] = mixed
        normed_v[rows, :] = norm(mixed.astype(F32)).astype(BF)

    loads[1].wait()

    @pl.loop(0, 16)
    def _(n):
        lanes = pl.ds(pl.multiple_of(n * 256, 256), 256)
        hidden = jnp.dot(normed_v[...], up_v[:, lanes], preferred_element_type=F32)
        hidden_v[:, lanes] = gelu(hidden).astype(BF)

    loads[2].wait()

    @pl.loop(0, 4)
    def _(pi):
        rows = pl.ds(pl.multiple_of(pi * 128, 128), 128)
        summed = jnp.dot(hidden_v[rows, :], down_v[...], preferred_element_type=F32)
        encoded = norm(tokens_v[rows, :].astype(F32) + summed)
        total = jnp.sum(encoded.reshape(16, 8, 1024), axis=0)
        pooled_v[pl.ds(pl.multiple_of(pi * 8, 8), 8), :] = total * 0.0625

    sc_v[...] = jnp.dot(pooled_v[...].astype(BF), head_ref[...], preferred_element_type=F32)
    for s in range(32):
        line = sc_v[pl.ds(patch_ref[s], 1), :]
        score_ref[pl.ds(s, 1), :] = jnp.where(s < count_ref[0], line, 0.0)

    pltpu.make_async_copy(fo, feat_hbm, fsem).wait()


def classify(p, first, rest, patch, count, pos, mix, head, embed, up, down):
    vm = pl.BlockSpec(memory_space=pltpu.VMEM)
    sm = pl.BlockSpec(memory_space=pltpu.SMEM)
    hb = pl.BlockSpec(memory_space=pl.ANY)
    return pl.pallas_call(
        main_kernel,
        out_shape=(
            jax.ShapeDtypeStruct((64, 128, 128), BF),
            jax.ShapeDtypeStruct((32, 8), F32),
        ),
        in_specs=[vm, vm, vm, sm, sm, vm, vm, vm, hb, hb, hb],
        out_specs=(hb, vm),
        scratch_shapes=[
            pltpu.VMEM((256, 768), BF),
            pltpu.VMEM((3, 256, 1536), BF),
            pltpu.VMEM((35, Q, S, 256), BF),
            pltpu.VMEM((34, Q, S, 256), BF),
            pltpu.VMEM((8, COLS, 128), F32),
            pltpu.VMEM((64, 128, 128), BF),
            pltpu.VMEM((512, 2048), BF),
            pltpu.VMEM((2048, 1024), BF),
            pltpu.VMEM((1024, 4096), BF),
            pltpu.VMEM((4096, 1024), BF),
            pltpu.VMEM((512, 1024), BF),
            pltpu.VMEM((512, 1024), BF),
            pltpu.VMEM((512, 4096), BF),
            pltpu.VMEM((32, 1024), F32),
            pltpu.VMEM((32, 8), F32),
            pltpu.SemaphoreType.DMA((3,)),
            pltpu.SemaphoreType.DMA,
        ],
        compiler_params=pltpu.CompilerParams(vmem_limit_bytes=60 * 2**20),
        name="classify",
    )(p, first, rest, patch, count, pos, mix, head, embed, up, down)


def on_device(input_field, conv_first, conv_rest, flag_patch, flag_count, w_embed, pos_embed,
              token_mix, w_up, w_down, w_head):
    p = exchange(input_field)
    features, scores = classify(
        p, conv_first.reshape(9, 128, 64), conv_rest.reshape(27, 128, 128),
        flag_patch.reshape(32), flag_count.reshape(1), pos_embed, token_mix, w_head,
        w_embed, w_up, w_down,
    )
    return (features, scores[None, None])


def solution(mesh):
    placed = (
        P(None, "lat", "lon"), P(), P(), P("lat", "lon", None), P("lat", "lon"),
        P(), P(), P(), P(), P(), P(),
    )
    return jax.shard_map(
        on_device,
        mesh=mesh,
        in_specs=placed,
        out_specs=(P("lat", "lon", None), P("lat", "lon", None, None)),
        check_vma=False,
    )
```

profile of v0, /device:TPU:1, one launch (start us, length us, event | category | flops | bytes accessed | tf_op | source)
XLA Modules:
  0.0 71.7 jit_solution(11738370461316894035)
XLA Ops:
  1.3 1.6 %copy.14.head_ref = bf16[1024,8]{1,0:T(8,128)(2,1)} copy(bf16[1024,8]{0,1:T(8,128)(2,1)} %param.21) | data formatting | bytes 32768 | tf_op args[10]
  2.8 1.8 %copy.13 = bf16[3,3,128,64]{3,2,1,0:T(8,128)(2,1)} copy(bf16[3,3,128,64]{2,3,1,0:T(8,128)(2,1)} %param.12) | data formatting | bytes 294912 | tf_op args[1]
  4.6 0.0 copy-start.1
  4.6 1.2 %copy-done.1 = bf16[64,64,128]{2,1,0:T(8,128)(2,1)S(1)} copy-done((bf16[64,64,128]{2,1,0:T(8,128)(2,1)S(1)}, bf16[64,64,128]{2,1,0:T(8,128)(2,1)}, u32[]{:S(2)}) %copy-start.1) | copy-done | bytes 1048600
  5.8 18.9 %halo.1.p_ref = bf16[36,11,16,128]{3,2,1,0:T(8,128)(2,1)S(1)} custom-call(bf16[64,64,128]{2,1,0:T(8,128)(2,1)S(1)} %copy-done.1), custom_call_target="tpu_custom_call" | custom-call | tf_op jit(solution)/shard_map/halo/pallas_call | solution.py:130
  24.7 0.0 copy-start
  24.7 1.2 %copy-done = bf16[36,11,16,128]{3,2,1,0:T(8,128)(2,1)} copy-done((bf16[36,11,16,128]{3,2,1,0:T(8,128)(2,1)}, bf16[36,11,16,128]{3,2,1,0:T(8,128)(2,1)S(1)}, u32[]{:S(2)}) %copy-start) | copy-done | bytes 1622040
  25.9 44.5 %classify.1 = (bf16[64,128,128]{2,1,0:T(8,128)(2,1)}, f32[32,8]{1,0:T(8,128)}) custom-call(bf16[36,11,16,128]{3,2,1,0:T(8,128)(2,1)} %copy-done, bf16[9,128,64]{2,1,0:T(8,128)(2,1)} %bitcast.6, bf16[27,128,128]{2,1,0:T(8,128)(2,1)} %bitcast.7, s32[32]{0:T(128)} %bitcast.9, s32[1]{0:T(128)} %bitcast.5.count_ref, bf16[16,1024]{1,0:T(8,128)(2,1)} %pos_ref.1, ...), custom_call_target="tpu_custom_call" | custom-call | tf_op jit(solution)/shard_map/classify/pallas_call | solution.py:332
  70.4 1.4 %copy.15 = f32[1,1,32,8]{2,3,1,0:T(8,128)} copy(f32[1,1,32,8]{3,2,1,0:T(8,128)} %bitcast.8) | data formatting | bytes 2048
Async XLA Ops:
  4.6 1.2 %copy-start.1 = (bf16[64,64,128]{2,1,0:T(8,128)(2,1)S(1)}, bf16[64,64,128]{2,1,0:T(8,128)(2,1)}, u32[]{:S(2)}) copy-start(bf16[64,64,128]{2,1,0:T(8,128)(2,1)} %x_ref.1) | copy-start | bytes 3145732
  24.7 1.2 %copy-start = (bf16[36,11,16,128]{3,2,1,0:T(8,128)(2,1)}, bf16[36,11,16,128]{3,2,1,0:T(8,128)(2,1)S(1)}, u32[]{:S(2)}) copy-start(bf16[36,11,16,128]{3,2,1,0:T(8,128)(2,1)S(1)} %halo.1.p_ref) | copy-start | bytes 4866052
where the time goes:
time: 72.1 us; the launch traced here: 71.7 us
  Pallas kernels  63.3 us (88%)
  local copies, waits for them, and re-layouts  7.1 us (10%)
  between operations  1.3 us (2%)
    pallas_call x1, Pallas kernels, classify(): pl.pallas_call(main_kernel, out_shape=(jax.ShapeDtypeStruct((64, 128, 128...  44.5 us
    pallas_call x1, Pallas kernels, exchange(): pl.pallas_call(halo_kernel, out_shape=jax.ShapeDtypeStruct((36, Q, S, 128...  18.9 us
    unnamed x7, local copies, waits for them, and re-layouts  7.1 us

commit v1 on v0

v1 whole, which is shorter than its diff:
```python
import functools

import jax
import jax.numpy as jnp
from jax import lax
from jax.experimental import pallas as pl
from jax.experimental.pallas import tpu as pltpu
from jax.sharding import PartitionSpec as P

BF = jnp.bfloat16
F32 = jnp.float32
MESH = pl.DeviceIdType.MESH

W = 8
Q = W + 2
S = 16
COLS = W * S
STRIP = 48
HELD = 56
NEG = (((1,), (1,)), ((), ()))
POS = (((1,), (0,)), ((), ()))


def silu(v):
    half = 0.5 * v
    return half + half * jnp.tanh(half)


def gelu(v):
    v = v.astype(BF)
    half = BF(0.5) * v
    return half + half * jnp.tanh(v * (BF(0.7978845608028654) + BF(0.035677408136300125) * (v * v)))


def norm(v):
    centred = v - jnp.mean(v, axis=-1, keepdims=True)
    return centred * lax.rsqrt(jnp.mean(centred * centred, axis=-1, keepdims=True) + 1e-05)


def conv_kernel(x_hbm, first_hbm, rest_hbm, embed_hbm, fo, tok, embed_v, x_ref, first_ref, rest_ref, xf, x0, x1, x2, x3, f4, wt1, wts,
                colf, col_l, col_r, sf0, sf1, sf2, sf3, r_right, r_left, r_br, r_bl, r_tr, r_tl,
                send_sem, recv_sem, load_sem):
    loads = [
        pltpu.make_async_copy(x_hbm, x_ref, load_sem.at[0]),
        pltpu.make_async_copy(first_hbm, first_ref, load_sem.at[1]),
        pltpu.make_async_copy(rest_hbm, rest_ref, load_sem.at[2]),
        pltpu.make_async_copy(embed_hbm, embed_v, load_sem.at[3]),
    ]
    for load in loads:
        load.start()
    lon = lax.axis_index("lon")
    lat = lax.axis_index("lat")
    n_lon = lax.axis_size("lon")
    n_lat = lax.axis_size("lat")
    west = lax.rem(lon + n_lon - 1, n_lon)
    east = lax.rem(lon + 1, n_lon)
    north = lax.rem(lat + n_lat - 1, n_lat)
    south = lax.rem(lat + 1, n_lat)
    barrier = pltpu.get_barrier_semaphore()
    places = ((lon, north), (lon, south), (west, lat), (east, lat),
              (west, north), (east, north), (west, south), (east, south))
    for place in places:
        pl.semaphore_signal(barrier, inc=1, device_id=place, device_id_type=MESH)
    low = jnp.where(lat == 0, 0, -64)
    high = jnp.where(lat == n_lat - 1, 64, 128)

    loads[0].wait()
    xf[...] = x_ref[...].astype(F32).reshape(64 * 64, 128)
    mm = lax.broadcasted_iota(jnp.int32, (Q * S, 128), 0)
    jj = lax.broadcasted_iota(jnp.int32, (Q * S, 128), 1)
    order = (jj == mm % S * W + mm // S - 1).astype(BF)

    def turn(k):
        rows = jnp.concatenate(
            [xf[pl.ds(2 * k + i, 64, 64), :] for i in range(4)], axis=0
        ).astype(BF)
        cells = lax.dot_general(order, rows, NEG, preferred_element_type=F32)
        for h in range(2):
            own = cells[:, h * 128:h * 128 + 128].reshape(Q, S, 128)
            x0[k + 2 + h] = own.astype(BF)
            for c in range(4):
                colf[0, c, pl.ds(k + h, 1), :] = own[c + 1, 0:1]
                colf[1, c, pl.ds(k + h, 1), :] = own[c + 5, 15:16]
            for c in range(2):
                sf0[0, 4 + c, pl.ds(k + 2 + h, 1), :] = own[c + 1, 0:1]
                sf0[1, c, pl.ds(k + 2 + h, 1), :] = own[c + 7, 15:16]

    @pl.loop(0, 16, unroll=2)
    def _(k):
        turn(2 * k)

    col_l[...] = colf[0].astype(BF)
    col_r[...] = colf[1].astype(BF)

    loads[1].wait()
    loads[2].wait()
    for ro in range(2):
        out = slice(ro * 128, ro * 128 + 128)
        for p in range(2):
            for dq in range(3):
                for half in range(2):
                    a = 2 * p + half - ro
                    at = (p * 3 + dq) * 2 + half
                    wt1[at * 64:at * 64 + 64, out] = (
                        first_ref[a * 3 + dq] if 0 <= a < 3 else jnp.zeros((64, 128), BF)
                    )
                    for l in range(3):
                        wts[l, out, at * 128:at * 128 + 128] = (
                            rest_ref[l * 9 + a * 3 + dq] if 0 <= a < 3 else jnp.zeros((128, 128), BF)
                        )

    xs = (x0, x1, x2, x3)
    sfs = (sf0, sf1, sf2, sf3)

    def taps(l):
        return (wt1[...], POS) if l == 1 else (wts[l - 2], NEG)

    def rows_of(src, k, r):
        slabs = []
        for p in range(2):
            for dq in range(3):
                part = src[pl.ds(k + p, r), dq:dq + W]
                slabs.append(part.reshape(r * COLS, part.shape[-1]))
        return jnp.concatenate(slabs, axis=1)

    def keep(l, k, y, border):
        n = y.shape[0]
        if border and l < 4:
            pair = lax.broadcasted_iota(jnp.int32, (n, 1, 1, 256), 0)
            lane = lax.broadcasted_iota(jnp.int32, (n, 1, 1, 256), 3)
            row = l - 4 + 2 * (k + pair) + lane // 128
            y = jnp.where((row >= low) & (row < high), y, 0.0)
        if l == 4:
            for i in range(n):
                for half in range(2):
                    for q in range(W):
                        f4[pl.ds((2 * (k + i) + half) * COLS + q, S, W), :] = (
                            y[i, q, :, half * 128:half * 128 + 128]
                        )
            return
        dst = xs[l]
        dst[pl.ds(k, n), 1:W + 1] = y.astype(BF)
        sf = sfs[l]
        for i in range(n):
            dst[k + i, 0] = pltpu.roll(y[i, W - 1], 1, 0).astype(BF)
            dst[k + i, W + 1] = pltpu.roll(y[i, 0], S - 1, 0).astype(BF)
            for c in range(2):
                sf[0, 4 + c, pl.ds(k + i, 1), :] = y[i, l + c, 0:1]
                sf[1, c, pl.ds(k + i, 1), :] = y[i, W - 2 - l + c, S - 1:S]

    def main(l, k, r, border=False):
        weights, dims = taps(l)
        summed = lax.dot_general(rows_of(xs[l - 1], k, r), weights, dims, preferred_element_type=F32)
        keep(l, k, silu(summed).reshape(r, W, S, 256), border)

    def inner(l, r, first=0, last=None):
        pairs = 32 - l
        steps = (pairs + r - 1) // r

        @pl.loop(first, steps if last is None else last)
        def _(step):
            main(l, jnp.minimum(2 + step * r, 2 + pairs - r), r)

    inner(1, 8)
    inner(2, 10, 0, 1)

    pl.semaphore_wait(barrier, 8)
    sends = (
        (x0.at[2:4], x0.at[34:36]), (x0.at[32:34], x0.at[0:2]), (col_l, r_right), (col_r, r_left),
        (col_l.at[:, 0:16], r_br), (col_r.at[:, 0:16], r_bl),
        (col_l.at[:, 16:32], r_tr), (col_r.at[:, 16:32], r_tl),
    )
    copies = []
    for i, ((src, dst), place) in enumerate(zip(sends, places)):
        copies.append(pltpu.make_async_remote_copy(
            src_ref=src, dst_ref=dst, send_sem=send_sem.at[i], recv_sem=recv_sem.at[i],
            device_id=place, device_id_type=MESH,
        ))
        copies[-1].start()

    inner(2, 10, 1)
    inner(3, 10)
    inner(4, 7)

    loads[3].wait()
    for copy in copies:
        copy.wait()

    @pl.when(lat == 0)
    def _():
        x0[0:2] = jnp.zeros((2, Q, S, 128), BF)

    @pl.when(lat == n_lat - 1)
    def _():
        x0[34:36] = jnp.zeros((2, Q, S, 128), BF)

    sf0[0, 0:4, 2:34, :] = r_left[...].astype(F32)
    sf0[1, 2:6, 2:34, :] = r_right[...].astype(F32)
    sf0[0, 0:4, 0:2, :] = r_tl[...].astype(F32)[:, 14:16]
    sf0[1, 2:6, 0:2, :] = r_tr[...].astype(F32)[:, 14:16]
    sf0[0, 0:4, 34:36, :] = r_bl[...].astype(F32)[:, 0:2]
    sf0[1, 2:6, 34:36, :] = r_br[...].astype(F32)[:, 0:2]
    for k in (0, 1, 34, 35):
        for c in range(2):
            sf0[0, 4 + c, k:k + 1, :] = x0[k, c + 1].astype(F32)[0:1]
            sf0[1, c, k:k + 1, :] = x0[k, c + 7].astype(F32)[15:16]

    @pl.when(lat == 0)
    def _():
        sf0[:, :, 0:2, :] = jnp.zeros((2, 6, 2, 128), F32)

    @pl.when(lat == n_lat - 1)
    def _():
        sf0[:, :, 34:36, :] = jnp.zeros((2, 6, 2, 128), F32)

    def strips(l):
        src = sfs[l - 1]
        wide = src.shape[-1]
        weights, dims = taps(l)
        slabs = []
        for p in range(2):
            for dq in range(3):
                part = src[:, dq:dq + 4, p:p + STRIP, :].astype(BF)
                slabs.append(part.reshape(8 * STRIP, wide))
        summed = lax.dot_general(jnp.concatenate(slabs, axis=1), weights, dims,
                                 preferred_element_type=F32)
        y = silu(summed).reshape(2, 4, STRIP, 256)
        if l == 4:
            for side in range(2):
                for c in range(4):
                    for half in range(2):
                        f4[pl.ds(half * COLS + 124 * side + c, 32, 2 * COLS), :] = (
                            y[side, c, 0:32, half * 128:half * 128 + 128]
                        )
            return
        pair = lax.broadcasted_iota(jnp.int32, (1, 1, STRIP, 256), 2)
        lane = lax.broadcasted_iota(jnp.int32, (1, 1, STRIP, 256), 3)
        row = l - 4 + 2 * pair + lane // 128
        y = jnp.where((row >= low) & (row < high), y, 0.0)
        sfs[l][0, 0:4, 0:STRIP, :] = y[0]
        sfs[l][1, 2:6, 0:STRIP, :] = y[1]

    for l in range(1, 5):
        main(l, 0, 2, True)
        main(l, 34 - l, 2, True)
        strips(l)

    @pl.loop(0, 16)
    def _(tr):
        for u in range(4):
            row = pl.multiple_of((tr * 4 + u) * COLS, COLS)
            fo[tr * 4 + u] = f4[pl.ds(row, COLS), :].astype(BF)
            for b2 in range(2):
                at = pl.multiple_of(tr * 32 + b2 * 16, 16)
                for v in range(4):
                    two = [f4[pl.ds(row + 4 * (2 * b2 + b) + v, 8, 16), :] for b in range(2)]
                    lane = (u * 4 + v) * 128
                    tok[pl.ds(at, 16), lane:lane + 128] = jnp.concatenate(two, axis=0).astype(BF)


def convolve(x, first, rest, embed):
    vm = pl.BlockSpec(memory_space=pltpu.VMEM)
    hb = pl.BlockSpec(memory_space=pltpu.HBM)
    side = pltpu.VMEM((4, 32, 128), BF)
    corner = pltpu.VMEM((4, 16, 128), BF)
    return pl.pallas_call(
        conv_kernel,
        out_shape=(
            jax.ShapeDtypeStruct((64, 128, 128), BF),
            jax.ShapeDtypeStruct((512, 2048), BF),
            jax.ShapeDtypeStruct((2048, 1024), BF),
        ),
        in_specs=[hb, hb, hb, hb],
        out_specs=(vm, vm, vm),
        scratch_shapes=[
            pltpu.VMEM((64, 64, 128), BF),
            pltpu.VMEM((9, 64, 128), BF),
            pltpu.VMEM((27, 128, 128), BF),
            pltpu.VMEM((64 * 64, 128), F32),
            pltpu.VMEM((36, Q, S, 128), BF),
            pltpu.VMEM((35, Q, S, 256), BF),
            pltpu.VMEM((34, Q, S, 256), BF),
            pltpu.VMEM((33, Q, S, 256), BF),
            pltpu.VMEM((64 * 128, 128), F32),
            pltpu.VMEM((768, 256), BF),
            pltpu.VMEM((3, 256, 1536), BF),
            pltpu.VMEM((2, 4, 32, 128), F32),
            side, side,
            pltpu.VMEM((2, 6, HELD, 128), F32),
            pltpu.VMEM((2, 6, HELD, 256), F32),
            pltpu.VMEM((2, 6, HELD, 256), F32),
            pltpu.VMEM((2, 6, HELD, 256), F32),
            side, side, corner, corner, corner, corner,
            pltpu.SemaphoreType.DMA((8,)),
            pltpu.SemaphoreType.DMA((8,)),
            pltpu.SemaphoreType.DMA((4,)),
        ],
        compiler_params=pltpu.CompilerParams(
            collective_id=0, has_side_effects=True, vmem_limit_bytes=36 * 2**20
        ),
        name="convolve",
    )(*in_hbm(x, first, rest, embed))


def token_kernel(tok, fo, embed_v, count_ref, patch_hbm, pos_hbm, mix_hbm, head_hbm, up_hbm, down_hbm,
                 feat_hbm, score_ref, patch_ref, pos_ref, mix_ref, head_ref,
                 up_v, down_v, tokens_v, normed_v, hidden_v, pooled_v, sc_v, wsem, fsem):
    pairs = (
        (pos_hbm, pos_ref), (up_hbm, up_v), (down_hbm, down_v), (mix_hbm, mix_ref),
        (head_hbm, head_ref), (patch_hbm, patch_ref),
    )
    loads = [pltpu.make_async_copy(src, dst, wsem.at[i]) for i, (src, dst) in enumerate(pairs)]
    for i in (0, 3, 4, 5, 1, 2):
        loads[i].start()
    feat_copy = pltpu.make_async_copy(fo, feat_hbm, fsem)
    feat_copy.start()

    loads[0].wait()

    @pl.loop(0, 2)
    def _(n):
        lanes = pl.ds(pl.multiple_of(n * 512, 512), 512)
        summed = jnp.dot(tok[...], embed_v[:, lanes], preferred_element_type=F32)
        place = pos_ref[:, lanes].astype(F32)
        wide = summed.reshape(4, 16, 8, 512) + place[None, :, None, :]
        tokens_v[:, lanes] = wide.reshape(512, 512).astype(BF)

    loads[3].wait()
    ti = lax.broadcasted_iota(jnp.int32, (128, 16), 0) // 8
    tj = lax.broadcasted_iota(jnp.int32, (128, 16), 1)
    pick = (ti == tj).astype(BF)
    spread = jnp.dot(pick, mix_ref[...], preferred_element_type=F32).astype(BF)
    spread = lax.dot_general(spread, pick, NEG, preferred_element_type=F32)
    ri = lax.broadcasted_iota(jnp.int32, (128, 128), 0) % 8
    rj = lax.broadcasted_iota(jnp.int32, (128, 128), 1) % 8
    mix = jnp.where(ri == rj, spread, 0.0).astype(BF)

    @pl.loop(0, 4, unroll=2)
    def _(pi):
        rows = pl.ds(pl.multiple_of(pi * 128, 128), 128)
        wide = tokens_v[rows, :].astype(F32)
        mixing = jnp.dot(mix, norm(wide).astype(BF), preferred_element_type=F32)
        mixed = (wide + mixing).astype(BF)
        tokens_v[rows, :] = mixed
        normed_v[rows, :] = norm(mixed.astype(F32)).astype(BF)

    loads[1].wait()

    @pl.loop(0, 4)
    def _(n):
        lanes = pl.ds(pl.multiple_of(n * 1024, 1024), 1024)
        hidden = jnp.dot(normed_v[...], up_v[:, lanes], preferred_element_type=F32)
        hidden_v[:, lanes] = gelu(hidden)

    loads[2].wait()

    @pl.loop(0, 2)
    def _(pi):
        rows = pl.ds(pl.multiple_of(pi * 256, 256), 256)
        summed = jnp.dot(hidden_v[rows, :], down_v[...], preferred_element_type=F32)
        encoded = norm(tokens_v[rows, :].astype(F32) + summed)
        total = jnp.sum(encoded.reshape(2, 16, 8, 1024), axis=1)
        pooled_v[pl.ds(pl.multiple_of(pi * 16, 16), 16), :] = total.reshape(16, 1024) * 0.0625

    for load in loads[4:]:
        load.wait()
    sc_v[0, :, 0:8] = lax.dot_general(
        pooled_v[...].astype(BF), head_ref[...], NEG, preferred_element_type=F32
    )
    for s in range(32):
        line = sc_v[0, pl.ds(patch_ref[0, 0, s], 1), :]
        sc_v[1, pl.ds(s, 1), :] = jnp.where(s < count_ref[0, 0], line, 0.0)
    score_ref[...] = jnp.transpose(sc_v[1], (1, 0))[0:8]
    feat_copy.wait()


def classify(tok, fo, embed, patch, count, pos, mix, head, up, down):
    vm = pl.BlockSpec(memory_space=pltpu.VMEM)
    hb = pl.BlockSpec(memory_space=pltpu.HBM)
    return pl.pallas_call(
        token_kernel,
        out_shape=(
            jax.ShapeDtypeStruct((64, 128, 128), BF),
            jax.ShapeDtypeStruct((8, 32), F32),
        ),
        in_specs=[vm, vm, vm, pl.BlockSpec(memory_space=pltpu.SMEM)] + [hb] * 6,
        out_specs=(hb, vm),
        scratch_shapes=[
            pltpu.SMEM((1, 1, 32), jnp.int32),
            pltpu.VMEM((16, 1024), BF),
            pltpu.VMEM((16, 16), BF),
            pltpu.VMEM((8, 1024), BF),
            pltpu.VMEM((1024, 4096), BF),
            pltpu.VMEM((4096, 1024), BF),
            pltpu.VMEM((512, 1024), BF),
            pltpu.VMEM((512, 1024), BF),
            pltpu.VMEM((512, 4096), BF),
            pltpu.VMEM((32, 1024), F32),
            pltpu.VMEM((2, 32, 128), F32),
            pltpu.SemaphoreType.DMA((6,)),
            pltpu.SemaphoreType.DMA,
        ],
        compiler_params=pltpu.CompilerParams(vmem_limit_bytes=40 * 2**20),
        name="classify",
    )(tok, fo, embed, count, *in_hbm(patch, pos, mix, head, up, down))


def in_hbm(*arrays):
    return tuple(pltpu.with_memory_space_constraint(a, pltpu.HBM) for a in arrays)


def on_device(input_field, conv_first, conv_rest, flag_patch, flag_count, w_embed, pos_embed,
              token_mix, w_up, w_down, w_head):
    fo, tok, embed = convolve(
        input_field, jnp.transpose(conv_first, (0, 1, 3, 2)).reshape(9, 64, 128),
        conv_rest.reshape(27, 128, 128), w_embed,
    )
    features, scores = classify(
        tok, fo, embed, flag_patch, flag_count, pos_embed, token_mix, w_head.T, w_up, w_down,
    )
    return (features, scores.T[None, None])


def solution(mesh):
    placed = (
        P(None, "lat", "lon"), P(), P(), P("lat", "lon", None), P("lat", "lon"),
        P(), P(), P(), P(), P(), P(),
    )
    return jax.shard_map(
        on_device,
        mesh=mesh,
        in_specs=placed,
        out_specs=(P("lat", "lon", None), P("lat", "lon", None, None)),
        check_vma=False,
    )
```

time: 72.1 us -> 45.9 us (0.64)
  Pallas kernels: 63.3 us -> 44.3 us
  local copies, waits for them, and re-layouts: 7.1 us -> 0 us
    pallas_call x2, Pallas kernels: 63.3 us -> 44.3 us  [the longest x1 26.9 us: convolve(): pl.pallas_call(conv_kernel, out_shape=(jax.ShapeDtypeStruct((64, 128, 128...]
    unnamed x7 -> x0, local copies, waits for them, and re-layouts: 7.1 us -> none
where the time goes in v1:
time: 45.9 us; the launch traced here: 45.8 us
  Pallas kernels  44.3 us (97%)
  between operations  1.45 us (3%)
    pallas_call x1, Pallas kernels, convolve(): pl.pallas_call(conv_kernel, out_shape=(jax.ShapeDtypeStruct((64, 128, 128...  26.9 us
    pallas_call x1, Pallas kernels, classify(): pl.pallas_call(token_kernel, out_shape=(jax.ShapeDtypeStruct((64, 128, 12...  17.4 us

profile of v1, /device:TPU:1, one launch (start us, length us, event | category | flops | bytes accessed | tf_op | source)
XLA Modules:
  0.0 45.8 jit_solution(15599437117891347363)
XLA Ops:
  1.3 26.9 %convolve.1 = (bf16[64,128,128]{2,1,0:T(8,128)(2,1)S(1)}, bf16[512,2048]{1,0:T(8,128)(2,1)S(1)}, bf16[2048,1024]{1,0:T(8,128)(2,1)S(1)}) custom-call(bf16[64,64,128]{2,1,0:T(8,128)(2,1)} %x_hbm.1, bf16[9,64,128]{2,1,0:T(8,128)(2,1)} %bitcast.9, bf16[27,128,128]{2,1,0:T(8,128)(2,1)} %bitcast.8, bf16[2048,1024]{1,0:T(8,128)(2,1)} %embed_hbm.1), custom_call_target="tpu_custom_call" | custom-call | tf_op jit(solution)/shard_map/convolve/pallas_call | solution.py:266
  28.2 17.4 %classify.1 = (bf16[64,128,128]{2,1,0:T(8,128)(2,1)}, f32[8,32]{1,0:T(8,128)}) custom-call(bf16[512,2048]{1,0:T(8,128)(2,1)S(1)} %get-tuple-element.7.tok, bf16[64,128,128]{2,1,0:T(8,128)(2,1)S(1)} %get-tuple-element.8.fo, bf16[2048,1024]{1,0:T(8,128)(2,1)S(1)} %get-tuple-element.9.embed_v, s32[1,1]{1,0:T(1,128)S(6)} %copy.13.count_ref, ...), custom_call_target="tpu_custom_call" | custom-call | tf_op jit(solution)/shard_map/classify/pallas_call | solution.py:380

commit v2 on v1

--- a/solution.py
+++ b/solution.py
@@ -15,8 +15,8 @@
 Q = W + 2
 S = 16
 COLS = W * S
-STRIP = 48
-HELD = 56
+STRIP = 40
+HELD = 48
 NEG = (((1,), (1,)), ((), ()))
 POS = (((1,), (0,)), ((), ()))
 
@@ -37,8 +37,8 @@
     return centred * lax.rsqrt(jnp.mean(centred * centred, axis=-1, keepdims=True) + 1e-05)
 
 
-def conv_kernel(x_hbm, first_hbm, rest_hbm, embed_hbm, fo, tok, embed_v, x_ref, first_ref, rest_ref, xf, x0, x1, x2, x3, f4, wt1, wts,
-                colf, col_l, col_r, sf0, sf1, sf2, sf3, r_right, r_left, r_br, r_bl, r_tr, r_tl,
+def conv_kernel(x_hbm, first_hbm, rest_hbm, embed_hbm, fo, tok, embed_v, x_ref, first_ref, rest_ref, xf, x0, x1, x2, x3, f4, wt1, wm, we,
+                colf, cornf, corner, col_l, col_r, sf0, sf1, sf2, sf3, r_right, r_left, r_br, r_bl, r_tr, r_tl,
                 send_sem, recv_sem, load_sem):
     loads = [
         pltpu.make_async_copy(x_hbm, x_ref, load_sem.at[0]),
@@ -85,10 +85,16 @@
                 sf0[0, 4 + c, pl.ds(k + 2 + h, 1), :] = own[c + 1, 0:1]
                 sf0[1, c, pl.ds(k + 2 + h, 1), :] = own[c + 7, 15:16]
 
-    @pl.loop(0, 16, unroll=2)
+    @pl.loop(0, 16, unroll=4)
     def _(k):
         turn(2 * k)
 
+    cornf[...] = jnp.zeros((2, 2, 16, 128), F32)
+    for e in range(2):
+        for end in range(2):
+            for c in range(4):
+                cornf[e, end, 2 * c:2 * c + 2, :] = colf[e, c, 30 * end:30 * end + 2, :]
+    corner[...] = cornf[...].astype(BF)
     col_l[...] = colf[0].astype(BF)
     col_r[...] = colf[1].astype(BF)
 
@@ -104,54 +110,101 @@
                     wt1[at * 64:at * 64 + 64, out] = (
                         first_ref[a * 3 + dq] if 0 <= a < 3 else jnp.zeros((64, 128), BF)
                     )
-                    for l in range(3):
-                        wts[l, out, at * 128:at * 128 + 128] = (
-                            rest_ref[l * 9 + a * 3 + dq] if 0 <= a < 3 else jnp.zeros((128, 128), BF)
-                        )
+    for l in range(3):
+        for o in range(2):
+            out = slice(o * 128, o * 128 + 128)
+            for dq in range(3):
+                for i in range(2):
+                    at = (dq * 2 + i) * 128
+                    wm[l, out, at:at + 128] = rest_ref[l * 9 + (i + 1 - o) * 3 + dq]
+            for e in range(2):
+                for t in range(4):
+                    b = t - o
+                    we[l, e, out, t * 128:t * 128 + 128] = (
+                        rest_ref[l * 9 + 6 * e + b] if 0 <= b < 3 else jnp.zeros((128, 128), BF)
+                    )
 
     xs = (x0, x1, x2, x3)
     sfs = (sf0, sf1, sf2, sf3)
 
-    def taps(l):
-        return (wt1[...], POS) if l == 1 else (wts[l - 2], NEG)
-
-    def rows_of(src, k, r):
+    def product(l, groups):
+        def stack(p, first, step, *half):
+            return jnp.concatenate(
+                [get(p, c, *half) for get, n in groups for c in range(first, first + n, step)], axis=0
+            )
+
+        def split(whole, parts):
+            at = 0
+            for size, n in parts:
+                yield [whole[at + c * size:at + c * size + size] for c in range(n)]
+                at += size * n
+
+        sizes = [(get(0, 0).shape[0], n) for get, n in groups]
+        if l == 1:
+            slabs = [stack(p, dq, 1) for p in range(2) for dq in range(3)]
+            full = jnp.dot(jnp.concatenate(slabs, axis=1), wt1[...], preferred_element_type=F32)
+            return list(split(full, sizes))
         slabs = []
-        for p in range(2):
-            for dq in range(3):
-                part = src[pl.ds(k + p, r), dq:dq + W]
-                slabs.append(part.reshape(r * COLS, part.shape[-1]))
-        return jnp.concatenate(slabs, axis=1)
-
-    def keep(l, k, y, border):
-        n = y.shape[0]
-        if border and l < 4:
-            pair = lax.broadcasted_iota(jnp.int32, (n, 1, 1, 256), 0)
-            lane = lax.broadcasted_iota(jnp.int32, (n, 1, 1, 256), 3)
-            row = l - 4 + 2 * (k + pair) + lane // 128
-            y = jnp.where((row >= low) & (row < high), y, 0.0)
-        if l == 4:
-            for i in range(n):
-                for half in range(2):
-                    for q in range(W):
+        for dq in range(3):
+            slabs += [stack(0, dq, 1, 1), stack(1, dq, 1, 0)]
+        full = lax.dot_general(jnp.concatenate(slabs, axis=1), wm[l - 2], NEG, preferred_element_type=F32)
+        outer = []
+        for e in range(2):
+            slabs = [stack(e, t, 2, e) for t in range(4)]
+            part = lax.dot_general(
+                jnp.concatenate(slabs, axis=1), we[l - 2, e], NEG, preferred_element_type=F32
+            )
+            outer.append(list(split(part, [(size, n // 2) for size, n in sizes])))
+        sums = []
+        for g, columns in enumerate(split(full, sizes)):
+            for c in range(len(columns)):
+                lanes = slice(c % 2 * 128, c % 2 * 128 + 128)
+                columns[c] = columns[c] + jnp.concatenate(
+                    [part[g][c // 2][:, lanes] for part in outer], axis=1
+                )
+            sums.append(columns)
+        return sums
+
+    def inside(l, first, shape, dim):
+        pair = lax.broadcasted_iota(jnp.int32, shape, dim)
+        lane = lax.broadcasted_iota(jnp.int32, shape, len(shape) - 1)
+        row = l - 4 + 2 * (first + pair) + lane // 128
+        return (row >= low) & (row < high)
+
+    def of_main(l, k, r):
+        src = xs[l - 1]
+
+        def get(p, c, half=None):
+            lanes = slice(None) if half is None else slice(half * 128, half * 128 + 128)
+            part = src[pl.ds(k + p, r), c, :, lanes]
+            return part.reshape(r * S, part.shape[-1])
+
+        return get, W
+
+    def keep(l, k, r, sums, border=False):
+        for q in range(W):
+            y = silu(sums[q]).reshape(r, S, 256)
+            if border and l < 4:
+                y = jnp.where(inside(l, k, (r, S, 256), 0), y, 0.0)
+            if l == 4:
+                for i in range(r):
+                    for half in range(2):
                         f4[pl.ds((2 * (k + i) + half) * COLS + q, S, W), :] = (
-                            y[i, q, :, half * 128:half * 128 + 128]
+                            y[i, :, half * 128:half * 128 + 128]
                         )
-            return
-        dst = xs[l]
-        dst[pl.ds(k, n), 1:W + 1] = y.astype(BF)
-        sf = sfs[l]
-        for i in range(n):
-            dst[k + i, 0] = pltpu.roll(y[i, W - 1], 1, 0).astype(BF)
-            dst[k + i, W + 1] = pltpu.roll(y[i, 0], S - 1, 0).astype(BF)
-            for c in range(2):
-                sf[0, 4 + c, pl.ds(k + i, 1), :] = y[i, l + c, 0:1]
-                sf[1, c, pl.ds(k + i, 1), :] = y[i, W - 2 - l + c, S - 1:S]
-
-    def main(l, k, r, border=False):
-        weights, dims = taps(l)
-        summed = lax.dot_general(rows_of(xs[l - 1], k, r), weights, dims, preferred_element_type=F32)
-        keep(l, k, silu(summed).reshape(r, W, S, 256), border)
+                continue
+            dst = xs[l]
+            dst[pl.ds(k, r), q + 1] = y.astype(BF)
+            for i in range(r):
+                if q == W - 1:
+                    dst[k + i, 0] = pltpu.roll(y[i], 1, 0).astype(BF)
+                if q == 0:
+                    dst[k + i, W + 1] = pltpu.roll(y[i], S - 1, 0).astype(BF)
+                for c in range(2):
+                    if q == l + c:
+                        sfs[l][0, 4 + c, pl.ds(k + i, 1), :] = y[i, 0:1]
+                    if q == W - 2 - l + c:
+                        sfs[l][1, c, pl.ds(k + i, 1), :] = y[i, S - 1:S]
 
     def inner(l, r, first=0, last=None):
         pairs = 32 - l
@@ -159,16 +212,16 @@
 
         @pl.loop(first, steps if last is None else last)
         def _(step):
-            main(l, jnp.minimum(2 + step * r, 2 + pairs - r), r)
-
-    inner(1, 8)
-    inner(2, 10, 0, 1)
+            k = jnp.minimum(2 + step * r, 2 + pairs - r)
+            keep(l, k, r, product(l, [of_main(l, k, r)])[0])
+
+    inner(1, 16, 0, 1)
 
     pl.semaphore_wait(barrier, 8)
     sends = (
-        (x0.at[2:4], x0.at[34:36]), (x0.at[32:34], x0.at[0:2]), (col_l, r_right), (col_r, r_left),
-        (col_l.at[:, 0:16], r_br), (col_r.at[:, 0:16], r_bl),
-        (col_l.at[:, 16:32], r_tr), (col_r.at[:, 16:32], r_tl),
+        (x0.at[2:4, 1:W + 1], x0.at[34:36, 1:W + 1]), (x0.at[32:34, 1:W + 1], x0.at[0:2, 1:W + 1]),
+        (col_l, r_right), (col_r, r_left), (corner.at[0, 0], r_br), (corner.at[1, 0], r_bl),
+        (corner.at[0, 1], r_tr), (corner.at[1, 1], r_tl),
     )
     copies = []
     for i, ((src, dst), place) in enumerate(zip(sends, places)):
@@ -178,9 +231,10 @@
         ))
         copies[-1].start()
 
-    inner(2, 10, 1)
-    inner(3, 10)
-    inner(4, 7)
+    inner(1, 16, 1)
+    inner(2, 15)
+    inner(3, 15)
+    inner(4, 14)
 
     loads[3].wait()
     for copy in copies:
@@ -196,14 +250,20 @@
 
     sf0[0, 0:4, 2:34, :] = r_left[...].astype(F32)
     sf0[1, 2:6, 2:34, :] = r_right[...].astype(F32)
-    sf0[0, 0:4, 0:2, :] = r_tl[...].astype(F32)[:, 14:16]
-    sf0[1, 2:6, 0:2, :] = r_tr[...].astype(F32)[:, 14:16]
-    sf0[0, 0:4, 34:36, :] = r_bl[...].astype(F32)[:, 0:2]
-    sf0[1, 2:6, 34:36, :] = r_br[...].astype(F32)[:, 0:2]
-    for k in (0, 1, 34, 35):
-        for c in range(2):
-            sf0[0, 4 + c, k:k + 1, :] = x0[k, c + 1].astype(F32)[0:1]
-            sf0[1, c, k:k + 1, :] = x0[k, c + 7].astype(F32)[15:16]
+    for at, west_end, east_end in ((0, r_tl, r_tr), (34, r_bl, r_br)):
+        for e, end in enumerate((west_end, east_end)):
+            rows = end[...].astype(F32)
+            for c in range(4):
+                sf0[e, 2 * e + c, at:at + 2, :] = rows[2 * c:2 * c + 2]
+        for k in (at, at + 1):
+            first = x0[k, 1].astype(F32)
+            last = x0[k, W].astype(F32)
+            x0[k, 0] = pltpu.roll(last, 1, 0).astype(BF)
+            x0[k, W + 1] = pltpu.roll(first, S - 1, 0).astype(BF)
+            sf0[0, 4, k:k + 1, :] = first[0:1]
+            sf0[0, 5, k:k + 1, :] = x0[k, 2].astype(F32)[0:1]
+            sf0[1, 0, k:k + 1, :] = x0[k, W - 1].astype(F32)[S - 1:S]
+            sf0[1, 1, k:k + 1, :] = last[S - 1:S]
 
     @pl.when(lat == 0)
     def _():
@@ -213,39 +273,37 @@
     def _():
         sf0[:, :, 34:36, :] = jnp.zeros((2, 6, 2, 128), F32)
 
-    def strips(l):
+    def of_strips(l):
         src = sfs[l - 1]
-        wide = src.shape[-1]
-        weights, dims = taps(l)
-        slabs = []
-        for p in range(2):
-            for dq in range(3):
-                part = src[:, dq:dq + 4, p:p + STRIP, :].astype(BF)
-                slabs.append(part.reshape(8 * STRIP, wide))
-        summed = lax.dot_general(jnp.concatenate(slabs, axis=1), weights, dims,
-                                 preferred_element_type=F32)
-        y = silu(summed).reshape(2, 4, STRIP, 256)
-        if l == 4:
-            for side in range(2):
-                for c in range(4):
+
+        def get(p, c, half=None):
+            lanes = slice(None) if half is None else slice(half * 128, half * 128 + 128)
+            part = src[:, c, p:p + STRIP, lanes]
+            return part.reshape(2 * STRIP, part.shape[-1]).astype(BF)
+
+        return get, 4
+
+    def keep_strips(l, sums):
+        for c in range(4):
+            y = silu(sums[c]).reshape(2, STRIP, 256)
+            if l == 4:
+                for side in range(2):
                     for half in range(2):
                         f4[pl.ds(half * COLS + 124 * side + c, 32, 2 * COLS), :] = (
-                            y[side, c, 0:32, half * 128:half * 128 + 128]
+                            y[side, 0:32, half * 128:half * 128 + 128]
                         )
-            return
-        pair = lax.broadcasted_iota(jnp.int32, (1, 1, STRIP, 256), 2)
-        lane = lax.broadcasted_iota(jnp.int32, (1, 1, STRIP, 256), 3)
-        row = l - 4 + 2 * pair + lane // 128
-        y = jnp.where((row >= low) & (row < high), y, 0.0)
-        sfs[l][0, 0:4, 0:STRIP, :] = y[0]
-        sfs[l][1, 2:6, 0:STRIP, :] = y[1]
+                continue
+            y = jnp.where(inside(l, 0, (1, STRIP, 256), 1), y, 0.0)
+            for side in range(2):
+                sfs[l][side, 2 * side + c, 0:STRIP, :] = y[side]
 
     for l in range(1, 5):
-        main(l, 0, 2, True)
-        main(l, 34 - l, 2, True)
-        strips(l)
-
-    @pl.loop(0, 16)
+        top, bottom, sides = product(l, [of_main(l, 0, 2), of_main(l, 34 - l, 2), of_strips(l)])
+        keep(l, 0, 2, top, True)
+        keep(l, 34 - l, 2, bottom, True)
+        keep_strips(l, sides)
+
+    @pl.loop(0, 16, unroll=2)
     def _(tr):
         for u in range(4):
             row = pl.multiple_of((tr * 4 + u) * COLS, COLS)
@@ -262,7 +320,7 @@
     vm = pl.BlockSpec(memory_space=pltpu.VMEM)
     hb = pl.BlockSpec(memory_space=pltpu.HBM)
     side = pltpu.VMEM((4, 32, 128), BF)
-    corner = pltpu.VMEM((4, 16, 128), BF)
+    corner = pltpu.VMEM((16, 128), BF)
     return pl.pallas_call(
         conv_kernel,
         out_shape=(
@@ -283,8 +341,11 @@
             pltpu.VMEM((33, Q, S, 256), BF),
             pltpu.VMEM((64 * 128, 128), F32),
             pltpu.VMEM((768, 256), BF),
-            pltpu.VMEM((3, 256, 1536), BF),
+            pltpu.VMEM((3, 256, 768), BF),
+            pltpu.VMEM((3, 2, 256, 512), BF),
             pltpu.VMEM((2, 4, 32, 128), F32),
+            pltpu.VMEM((2, 2, 16, 128), F32),
+            pltpu.VMEM((2, 2, 16, 128), BF),
             side, side,
             pltpu.VMEM((2, 6, HELD, 128), F32),
             pltpu.VMEM((2, 6, HELD, 256), F32),
@@ -296,7 +357,7 @@
             pltpu.SemaphoreType.DMA((4,)),
         ],
         compiler_params=pltpu.CompilerParams(
-            collective_id=0, has_side_effects=True, vmem_limit_bytes=36 * 2**20
+            collective_id=0, has_side_effects=True, vmem_limit_bytes=40 * 2**20
         ),
         name="convolve",
     )(*in_hbm(x, first, rest, embed))
@@ -316,15 +377,6 @@
     feat_copy.start()
 
     loads[0].wait()
-
-    @pl.loop(0, 2)
-    def _(n):
-        lanes = pl.ds(pl.multiple_of(n * 512, 512), 512)
-        summed = jnp.dot(tok[...], embed_v[:, lanes], preferred_element_type=F32)
-        place = pos_ref[:, lanes].astype(F32)
-        wide = summed.reshape(4, 16, 8, 512) + place[None, :, None, :]
-        tokens_v[:, lanes] = wide.reshape(512, 512).astype(BF)
-
     loads[3].wait()
     ti = lax.broadcasted_iota(jnp.int32, (128, 16), 0) // 8
     tj = lax.broadcasted_iota(jnp.int32, (128, 16), 1)
@@ -335,32 +387,52 @@
     rj = lax.broadcasted_iota(jnp.int32, (128, 128), 1) % 8
     mix = jnp.where(ri == rj, spread, 0.0).astype(BF)
 
-    @pl.loop(0, 4, unroll=2)
-    def _(pi):
-        rows = pl.ds(pl.multiple_of(pi * 128, 128), 128)
-        wide = tokens_v[rows, :].astype(F32)
-        mixing = jnp.dot(mix, norm(wide).astype(BF), preferred_element_type=F32)
-        mixed = (wide + mixing).astype(BF)
-        tokens_v[rows, :] = mixed
-        normed_v[rows, :] = norm(mixed.astype(F32)).astype(BF)
-
-    loads[1].wait()
-
-    @pl.loop(0, 4)
-    def _(n):
+    def embed(h):
+        rows = slice(h * 256, h * 256 + 256)
+        summed = jnp.dot(tok[rows, :], embed_v[...], preferred_element_type=F32)
+        wide = summed.reshape(2, 16, 8, 1024) + pos_ref[...].astype(F32)[None, :, None, :]
+        tokens_v[rows, :] = wide.reshape(256, 1024).astype(BF)
+
+    def mixes(h):
+        for pi in (2 * h, 2 * h + 1):
+            rows = slice(pi * 128, pi * 128 + 128)
+            wide = tokens_v[rows, :].astype(F32)
+            mixing = jnp.dot(mix, norm(wide).astype(BF), preferred_element_type=F32)
+            mixed = (wide + mixing).astype(BF)
+            tokens_v[rows, :] = mixed
+            normed_v[rows, :] = norm(mixed.astype(F32)).astype(BF)
+
+    def widen(h, n):
+        rows = slice(h * 256, h * 256 + 256)
         lanes = pl.ds(pl.multiple_of(n * 1024, 1024), 1024)
-        hidden = jnp.dot(normed_v[...], up_v[:, lanes], preferred_element_type=F32)
-        hidden_v[:, lanes] = gelu(hidden)
-
-    loads[2].wait()
-
-    @pl.loop(0, 2)
-    def _(pi):
-        rows = pl.ds(pl.multiple_of(pi * 256, 256), 256)
+        hidden = jnp.dot(normed_v[rows, :], up_v[:, lanes], preferred_element_type=F32)
+        hidden_v[rows, lanes] = gelu(hidden)
+
+    def narrow(h):
+        rows = slice(h * 256, h * 256 + 256)
         summed = jnp.dot(hidden_v[rows, :], down_v[...], preferred_element_type=F32)
         encoded = norm(tokens_v[rows, :].astype(F32) + summed)
         total = jnp.sum(encoded.reshape(2, 16, 8, 1024), axis=1)
-        pooled_v[pl.ds(pl.multiple_of(pi * 16, 16), 16), :] = total.reshape(16, 1024) * 0.0625
+        pooled_v[h * 16:h * 16 + 16, :] = total.reshape(16, 1024) * 0.0625
+
+    embed(0)
+    embed(1)
+    mixes(0)
+    loads[1].wait()
+    widen(0, 0)
+    mixes(1)
+
+    @pl.loop(1, 4, unroll=3)
+    def _(n):
+        widen(0, n)
+
+    @pl.loop(0, 4, unroll=4)
+    def _(n):
+        widen(1, n)
+
+    loads[2].wait()
+    narrow(0)
+    narrow(1)
 
     for load in loads[4:]:
         load.wait()

time: 45.9 us -> 42.4 us (0.924)
  Pallas kernels: 44.3 us -> 40.8 us
    pallas_call x1, Pallas kernels: 17.4 us -> 15 us  [classify(): pl.pallas_call(token_kernel, out_shape=(jax.ShapeDtypeStruct((64, 128, 12...]
    pallas_call x1, Pallas kernels: 26.9 us -> 25.8 us  [convolve(): pl.pallas_call(conv_kernel, out_shape=(jax.ShapeDtypeStruct((64, 128, 128...]
where the time goes in v2:
time: 42.4 us; the launch traced here: 42.3 us
  Pallas kernels  40.8 us (96%)
  between operations  1.45 us (3%)
    pallas_call x1, Pallas kernels, convolve(): pl.pallas_call(conv_kernel, out_shape=(jax.ShapeDtypeStruct((64, 128, 128...  25.8 us
    pallas_call x1, Pallas kernels, classify(): pl.pallas_call(token_kernel, out_shape=(jax.ShapeDtypeStruct((64, 128, 12...  15 us

profile of v2, /device:TPU:1, one launch (start us, length us, event | category | flops | bytes accessed | tf_op | source)
XLA Modules:
  0.0 42.3 jit_solution(6004929737822828226)
XLA Ops:
  1.3 25.8 %convolve.1 = (bf16[64,128,128]{2,1,0:T(8,128)(2,1)S(1)}, bf16[512,2048]{1,0:T(8,128)(2,1)S(1)}, bf16[2048,1024]{1,0:T(8,128)(2,1)S(1)}) custom-call(bf16[64,64,128]{2,1,0:T(8,128)(2,1)} %x_hbm.1, bf16[9,64,128]{2,1,0:T(8,128)(2,1)} %bitcast.9, bf16[27,128,128]{2,1,0:T(8,128)(2,1)} %bitcast.8, bf16[2048,1024]{1,0:T(8,128)(2,1)} %embed_hbm.1), custom_call_target="tpu_custom_call" | custom-call | tf_op jit(solution)/shard_map/convolve/pallas_call | solution.py:324
  27.1 15.0 %classify.1 = (bf16[64,128,128]{2,1,0:T(8,128)(2,1)}, f32[8,32]{1,0:T(8,128)}) custom-call(bf16[512,2048]{1,0:T(8,128)(2,1)S(1)} %get-tuple-element.7.tok, bf16[64,128,128]{2,1,0:T(8,128)(2,1)S(1)} %get-tuple-element.8.fo, bf16[2048,1024]{1,0:T(8,128)(2,1)S(1)} %get-tuple-element.9.embed_v, s32[1,1]{1,0:T(1,128)S(6)} %copy.13.count_ref, ...), custom_call_target="tpu_custom_call" | custom-call | tf_op jit(solution)/shard_map/classify/pallas_call | solution.py:452

commit v3 on v2

--- a/solution.py
+++ b/solution.py
@@ -37,7 +37,7 @@
     return centred * lax.rsqrt(jnp.mean(centred * centred, axis=-1, keepdims=True) + 1e-05)
 
 
-def conv_kernel(x_hbm, first_hbm, rest_hbm, embed_hbm, fo, tok, embed_v, x_ref, first_ref, rest_ref, xf, x0, x1, x2, x3, f4, wt1, wm, we,
+def conv_kernel(x_hbm, first_hbm, rest_hbm, embed_hbm, f4, embed_v, x_ref, first_ref, rest_ref, xf, x0, x1, x2, x3, wt1, wm, we,
                 colf, cornf, corner, col_l, col_r, sf0, sf1, sf2, sf3, r_right, r_left, r_br, r_bl, r_tr, r_tl,
                 send_sem, recv_sem, load_sem):
     loads = [
@@ -46,7 +46,7 @@
         pltpu.make_async_copy(rest_hbm, rest_ref, load_sem.at[2]),
         pltpu.make_async_copy(embed_hbm, embed_v, load_sem.at[3]),
     ]
-    for load in loads:
+    for load in loads[:3]:
         load.start()
     lon = lax.axis_index("lon")
     lat = lax.axis_index("lat")
@@ -100,6 +100,7 @@
 
     loads[1].wait()
     loads[2].wait()
+    loads[3].start()
     for ro in range(2):
         out = slice(ro * 128, ro * 128 + 128)
         for p in range(2):
@@ -303,18 +304,6 @@
         keep(l, 34 - l, 2, bottom, True)
         keep_strips(l, sides)
 
-    @pl.loop(0, 16, unroll=2)
-    def _(tr):
-        for u in range(4):
-            row = pl.multiple_of((tr * 4 + u) * COLS, COLS)
-            fo[tr * 4 + u] = f4[pl.ds(row, COLS), :].astype(BF)
-            for b2 in range(2):
-                at = pl.multiple_of(tr * 32 + b2 * 16, 16)
-                for v in range(4):
-                    two = [f4[pl.ds(row + 4 * (2 * b2 + b) + v, 8, 16), :] for b in range(2)]
-                    lane = (u * 4 + v) * 128
-                    tok[pl.ds(at, 16), lane:lane + 128] = jnp.concatenate(two, axis=0).astype(BF)
-
 
 def convolve(x, first, rest, embed):
     vm = pl.BlockSpec(memory_space=pltpu.VMEM)
@@ -324,12 +313,11 @@
     return pl.pallas_call(
         conv_kernel,
         out_shape=(
-            jax.ShapeDtypeStruct((64, 128, 128), BF),
-            jax.ShapeDtypeStruct((512, 2048), BF),
+            jax.ShapeDtypeStruct((64 * 128, 128), F32),
             jax.ShapeDtypeStruct((2048, 1024), BF),
         ),
         in_specs=[hb, hb, hb, hb],
-        out_specs=(vm, vm, vm),
+        out_specs=(vm, vm),
         scratch_shapes=[
             pltpu.VMEM((64, 64, 128), BF),
             pltpu.VMEM((9, 64, 128), BF),
@@ -339,7 +327,6 @@
             pltpu.VMEM((35, Q, S, 256), BF),
             pltpu.VMEM((34, Q, S, 256), BF),
             pltpu.VMEM((33, Q, S, 256), BF),
-            pltpu.VMEM((64 * 128, 128), F32),
             pltpu.VMEM((768, 256), BF),
             pltpu.VMEM((3, 256, 768), BF),
             pltpu.VMEM((3, 2, 256, 512), BF),
@@ -363,18 +350,29 @@
     )(*in_hbm(x, first, rest, embed))
 
 
-def token_kernel(tok, fo, embed_v, count_ref, patch_hbm, pos_hbm, mix_hbm, head_hbm, up_hbm, down_hbm,
+def token_kernel(f4, embed_v, count_ref, patch_hbm, pos_hbm, mix_hbm, head_hbm, up_hbm, down_hbm,
                  feat_hbm, score_ref, patch_ref, pos_ref, mix_ref, head_ref,
-                 up_v, down_v, tokens_v, normed_v, hidden_v, pooled_v, sc_v, wsem, fsem):
+                 fo, tok, up_v, down_v, tokens_v, normed_v, hidden_v, pooled_v, sc_v, wsem, fsem):
     pairs = (
         (pos_hbm, pos_ref), (up_hbm, up_v), (down_hbm, down_v), (mix_hbm, mix_ref),
         (head_hbm, head_ref), (patch_hbm, patch_ref),
     )
     loads = [pltpu.make_async_copy(src, dst, wsem.at[i]) for i, (src, dst) in enumerate(pairs)]
-    for i in (0, 3, 4, 5, 1, 2):
+    for i in (0, 3, 4, 5, 1):
         loads[i].start()
     feat_copy = pltpu.make_async_copy(fo, feat_hbm, fsem)
-    feat_copy.start()
+
+    def gather(h):
+        for tr in range(8 * h, 8 * h + 8):
+            for u in range(4):
+                row = (tr * 4 + u) * COLS
+                fo[tr * 4 + u] = f4[row:row + COLS, :].astype(BF)
+                for b2 in range(2):
+                    at = tr * 32 + b2 * 16
+                    for v in range(4):
+                        two = [f4[pl.ds(row + 4 * (2 * b2 + b) + v, 8, 16), :] for b in range(2)]
+                        lane = (u * 4 + v) * 128
+                        tok[at:at + 16, lane:lane + 128] = jnp.concatenate(two, axis=0).astype(BF)
 
     loads[0].wait()
     loads[3].wait()
@@ -415,10 +413,14 @@
         total = jnp.sum(encoded.reshape(2, 16, 8, 1024), axis=1)
         pooled_v[h * 16:h * 16 + 16, :] = total.reshape(16, 1024) * 0.0625
 
+    gather(0)
     embed(0)
+    gather(1)
     embed(1)
     mixes(0)
     loads[1].wait()
+    loads[2].start()
+    feat_copy.start()
     widen(0, 0)
     mixes(1)
 
@@ -446,7 +448,7 @@
     feat_copy.wait()
 
 
-def classify(tok, fo, embed, patch, count, pos, mix, head, up, down):
+def classify(f4, embed, patch, count, pos, mix, head, up, down):
     vm = pl.BlockSpec(memory_space=pltpu.VMEM)
     hb = pl.BlockSpec(memory_space=pltpu.HBM)
     return pl.pallas_call(
@@ -455,13 +457,15 @@
             jax.ShapeDtypeStruct((64, 128, 128), BF),
             jax.ShapeDtypeStruct((8, 32), F32),
         ),
-        in_specs=[vm, vm, vm, pl.BlockSpec(memory_space=pltpu.SMEM)] + [hb] * 6,
+        in_specs=[vm, vm, pl.BlockSpec(memory_space=pltpu.SMEM)] + [hb] * 6,
         out_specs=(hb, vm),
         scratch_shapes=[
             pltpu.SMEM((1, 1, 32), jnp.int32),
             pltpu.VMEM((16, 1024), BF),
             pltpu.VMEM((16, 16), BF),
             pltpu.VMEM((8, 1024), BF),
+            pltpu.VMEM((64, 128, 128), BF),
+            pltpu.VMEM((512, 2048), BF),
             pltpu.VMEM((1024, 4096), BF),
             pltpu.VMEM((4096, 1024), BF),
             pltpu.VMEM((512, 1024), BF),
@@ -474,7 +478,7 @@
         ],
         compiler_params=pltpu.CompilerParams(vmem_limit_bytes=40 * 2**20),
         name="classify",
-    )(tok, fo, embed, count, *in_hbm(patch, pos, mix, head, up, down))
+    )(f4, embed, count, *in_hbm(patch, pos, mix, head, up, down))
 
 
 def in_hbm(*arrays):
@@ -483,12 +487,12 @@
 
 def on_device(input_field, conv_first, conv_rest, flag_patch, flag_count, w_embed, pos_embed,
               token_mix, w_up, w_down, w_head):
-    fo, tok, embed = convolve(
+    f4, embed = convolve(
         input_field, jnp.transpose(conv_first, (0, 1, 3, 2)).reshape(9, 64, 128),
         conv_rest.reshape(27, 128, 128), w_embed,
     )
     features, scores = classify(
-        tok, fo, embed, flag_patch, flag_count, pos_embed, token_mix, w_head.T, w_up, w_down,
+        f4, embed, flag_patch, flag_count, pos_embed, token_mix, w_head.T, w_up, w_down,
     )
     return (features, scores.T[None, None])
 

time: 42.4 us -> 41.4 us (0.976)
  Pallas kernels: 40.8 us -> 39.8 us
    pallas_call x1, Pallas kernels: 25.8 us -> 24.2 us  [convolve(): pl.pallas_call(conv_kernel, out_shape=(jax.ShapeDtypeStruct((64 * 128, 12...]
    pallas_call x1, Pallas kernels: 15 us -> 15.6 us  [classify(): pl.pallas_call(token_kernel, out_shape=(jax.ShapeDtypeStruct((64, 128, 12...]
where the time goes in v3:
time: 41.4 us; the launch traced here: 41.2 us
  Pallas kernels  39.8 us (96%)
  between operations  1.47 us (4%)
    pallas_call x1, Pallas kernels, convolve(): pl.pallas_call(conv_kernel, out_shape=(jax.ShapeDtypeStruct((64 * 128, 12...  24.2 us
    pallas_call x1, Pallas kernels, classify(): pl.pallas_call(token_kernel, out_shape=(jax.ShapeDtypeStruct((64, 128, 12...  15.6 us

profile of v3, /device:TPU:1, one launch (start us, length us, event | category | flops | bytes accessed | tf_op | source)
XLA Modules:
  0.0 41.2 jit_solution(12925704752237763227)
XLA Ops:
  1.3 24.2 %convolve.1 = (f32[8192,128]{1,0:T(8,128)S(1)}, bf16[2048,1024]{1,0:T(8,128)(2,1)S(1)}) custom-call(bf16[64,64,128]{2,1,0:T(8,128)(2,1)} %x_hbm.1, bf16[9,64,128]{2,1,0:T(8,128)(2,1)} %bitcast.9, bf16[27,128,128]{2,1,0:T(8,128)(2,1)} %bitcast.8, bf16[2048,1024]{1,0:T(8,128)(2,1)} %embed_hbm.1), custom_call_target="tpu_custom_call" | custom-call | tf_op jit(solution)/shard_map/convolve/pallas_call | solution.py:313
  25.5 15.6 %classify.1 = (bf16[64,128,128]{2,1,0:T(8,128)(2,1)}, f32[8,32]{1,0:T(8,128)}) custom-call(f32[8192,128]{1,0:T(8,128)S(1)} %get-tuple-element.6.f4, bf16[2048,1024]{1,0:T(8,128)(2,1)S(1)} %get-tuple-element.7.embed_v, s32[1,1]{1,0:T(1,128)S(6)} %copy.13.count_ref, s32[1,1,32]{2,1,0:T(1,128)} %patch_hbm.1, bf16[16,1024]{1,0:T(8,128)(2,1)} %pos_hbm.1, ...), custom_call_target="tpu_custom_call" | custom-call | tf_op jit(solution)/shard_map/classify/pallas_call | solution.py:454

commit v4 on v3

--- a/solution.py
+++ b/solution.py
@@ -59,8 +59,16 @@
     barrier = pltpu.get_barrier_semaphore()
     places = ((lon, north), (lon, south), (west, lat), (east, lat),
               (west, north), (east, north), (west, south), (east, south))
-    for place in places:
-        pl.semaphore_signal(barrier, inc=1, device_id=place, device_id_type=MESH)
+    to_north, to_south, level = (0, 4, 5), (1, 6, 7), (2, 3)
+    has_north, has_south = lat > 0, lat < n_lat - 1
+
+    def greet(those):
+        for i in those:
+            pl.semaphore_signal(barrier, inc=1, device_id=places[i], device_id_type=MESH)
+
+    greet(level)
+    pl.when(has_north)(lambda: greet(to_north))
+    pl.when(has_south)(lambda: greet(to_south))
     low = jnp.where(lat == 0, 0, -64)
     high = jnp.where(lat == n_lat - 1, 64, 128)
 
@@ -218,7 +226,9 @@
 
     inner(1, 16, 0, 1)
 
-    pl.semaphore_wait(barrier, 8)
+    surrounded = jnp.logical_and(has_north, has_south)
+    pl.when(surrounded)(lambda: pl.semaphore_wait(barrier, 8))
+    pl.when(jnp.logical_not(surrounded))(lambda: pl.semaphore_wait(barrier, 5))
     sends = (
         (x0.at[2:4, 1:W + 1], x0.at[34:36, 1:W + 1]), (x0.at[32:34, 1:W + 1], x0.at[0:2, 1:W + 1]),
         (col_l, r_right), (col_r, r_left), (corner.at[0, 0], r_br), (corner.at[1, 0], r_bl),
@@ -230,7 +240,22 @@
             src_ref=src, dst_ref=dst, send_sem=send_sem.at[i], recv_sem=recv_sem.at[i],
             device_id=place, device_id_type=MESH,
         ))
-        copies[-1].start()
+
+    def send(those):
+        for i in those:
+            copies[i].start()
+
+    def sent(those):
+        for i in those:
+            copies[i].wait_send()
+
+    def arrived(those):
+        for i in those:
+            copies[i].wait_recv()
+
+    pl.when(has_north)(lambda: send(to_north))
+    pl.when(has_south)(lambda: send(to_south))
+    send(level)
 
     inner(1, 16, 1)
     inner(2, 15)
@@ -238,8 +263,18 @@
     inner(4, 14)
 
     loads[3].wait()
-    for copy in copies:
-        copy.wait()
+    sent(level)
+    arrived(level)
+
+    @pl.when(has_north)
+    def _():
+        sent(to_north)
+        arrived(to_south)
+
+    @pl.when(has_south)
+    def _():
+        sent(to_south)
+        arrived(to_north)
 
     @pl.when(lat == 0)
     def _():

time: 41.4 us -> 38.3 us (0.925)
  Pallas kernels: 39.8 us -> 36.6 us
    pallas_call x1, Pallas kernels: 24.2 us -> 21.1 us  [convolve(): pl.pallas_call(conv_kernel, out_shape=(jax.ShapeDtypeStruct((64 * 128, 12...]
where the time goes in v4:
time: 38.3 us; the launch traced here: 38.1 us
  Pallas kernels  36.6 us (96%)
  between operations  1.47 us (4%)
    pallas_call x1, Pallas kernels, convolve(): pl.pallas_call(conv_kernel, out_shape=(jax.ShapeDtypeStruct((64 * 128, 12...  21.1 us
    pallas_call x1, Pallas kernels, classify(): pl.pallas_call(token_kernel, out_shape=(jax.ShapeDtypeStruct((64, 128, 12...  15.6 us

profile of v4, /device:TPU:1, one launch (start us, length us, event | category | flops | bytes accessed | tf_op | source)
XLA Modules:
  0.0 38.1 jit_solution(13052539742384266107)
XLA Ops:
  1.3 21.1 %convolve.1 = (f32[8192,128]{1,0:T(8,128)S(1)}, bf16[2048,1024]{1,0:T(8,128)(2,1)S(1)}) custom-call(bf16[64,64,128]{2,1,0:T(8,128)(2,1)} %x_hbm.1, bf16[9,64,128]{2,1,0:T(8,128)(2,1)} %bitcast.9, bf16[27,128,128]{2,1,0:T(8,128)(2,1)} %bitcast.8, bf16[2048,1024]{1,0:T(8,128)(2,1)} %embed_hbm.1), custom_call_target="tpu_custom_call" | custom-call | tf_op jit(solution)/shard_map/convolve/pallas_call | solution.py:348
  22.4 15.6 %classify.1 = (bf16[64,128,128]{2,1,0:T(8,128)(2,1)}, f32[8,32]{1,0:T(8,128)}) custom-call(f32[8192,128]{1,0:T(8,128)S(1)} %get-tuple-element.6.f4, bf16[2048,1024]{1,0:T(8,128)(2,1)S(1)} %get-tuple-element.7.embed_v, s32[1,1]{1,0:T(1,128)S(6)} %copy.13.count_ref, s32[1,1,32]{2,1,0:T(1,128)} %patch_hbm.1, bf16[16,1024]{1,0:T(8,128)(2,1)} %pos_hbm.1, ...), custom_call_target="tpu_custom_call" | custom-call | tf_op jit(solution)/shard_map/classify/pallas_call | solution.py:489

commit v5 on v4

--- a/solution.py
+++ b/solution.py
@@ -93,7 +93,7 @@
                 sf0[0, 4 + c, pl.ds(k + 2 + h, 1), :] = own[c + 1, 0:1]
                 sf0[1, c, pl.ds(k + 2 + h, 1), :] = own[c + 7, 15:16]
 
-    @pl.loop(0, 16, unroll=4)
+    @pl.loop(0, 16, unroll=16)
     def _(k):
         turn(2 * k)
 

time: 38.3 us -> 37.9 us (0.990)
  no operation moved by 1% of the time
where the time goes in v5:
time: 37.9 us; the launch traced here: 37.8 us
  Pallas kernels  36.3 us (96%)
  between operations  1.47 us (4%)
    pallas_call x1, Pallas kernels, convolve(): pl.pallas_call(conv_kernel, out_shape=(jax.ShapeDtypeStruct((64 * 128, 12...  20.8 us
    pallas_call x1, Pallas kernels, classify(): pl.pallas_call(token_kernel, out_shape=(jax.ShapeDtypeStruct((64, 128, 12...  15.6 us

profile of v5, /device:TPU:1, one launch (start us, length us, event | category | flops | bytes accessed | tf_op | source)
XLA Modules:
  0.0 37.8 jit_solution(1680855641595570500)
XLA Ops:
  1.3 20.8 %convolve.1 = (f32[8192,128]{1,0:T(8,128)S(1)}, bf16[2048,1024]{1,0:T(8,128)(2,1)S(1)}) custom-call(bf16[64,64,128]{2,1,0:T(8,128)(2,1)} %x_hbm.1, bf16[9,64,128]{2,1,0:T(8,128)(2,1)} %bitcast.9, bf16[27,128,128]{2,1,0:T(8,128)(2,1)} %bitcast.8, bf16[2048,1024]{1,0:T(8,128)(2,1)} %embed_hbm.1), custom_call_target="tpu_custom_call" | custom-call | tf_op jit(solution)/shard_map/convolve/pallas_call | solution.py:348
  22.0 15.6 %classify.1 = (bf16[64,128,128]{2,1,0:T(8,128)(2,1)}, f32[8,32]{1,0:T(8,128)}) custom-call(f32[8192,128]{1,0:T(8,128)S(1)} %get-tuple-element.6.f4, bf16[2048,1024]{1,0:T(8,128)(2,1)S(1)} %get-tuple-element.7.embed_v, s32[1,1]{1,0:T(1,128)S(6)} %copy.13.count_ref, s32[1,1,32]{2,1,0:T(1,128)} %patch_hbm.1, bf16[16,1024]{1,0:T(8,128)(2,1)} %pos_hbm.1, ...), custom_call_target="tpu_custom_call" | custom-call | tf_op jit(solution)/shard_map/classify/pallas_call | solution.py:489
